TPU v7x, 32 devices: a whole 2x2x4 slice. The times are simulated.
32 devices in a mesh: group: 2 (over x), row: 8 (over z, y), col: 2 (over core).
Axes of the slice: x: 2, y: 2, z: 4, core: 2. Of those that a mesh axis runs over, the one named last changes fastest.
Arguments:
- anomalies: bfloat16 [32, 65536], P('group', ('row', 'col')), parts along dimension 0, may hold values from -6 to 6
- order: int32 [16, 4096], P(('row', 'col')), may hold values from 0 to 4095, each once within a row
- bases: bfloat16 [256, 64, 256], P(('row', 'col')), may hold values from -0.375 to 0.375
- near_blocks: bfloat16 [256, 3, 256, 256], P(('row', 'col')), may hold values from -0.21875 to 0.21875
- far_rows: int32 [16, 256], P(('row', 'col')), may hold values from -1 to 255, as said below
- far_cols: int32 [16, 256], P(('row', 'col')), may hold values from -1 to 255, as said below
- coupling: bfloat16 [16, 256, 4096], P(('row', 'col')), may hold values from -0.75 to 0.75
Outputs:
- covaried: bfloat16 [32, 65536], P('group', ('row', 'col')), parts along dimension 0
There are 2 independent parts, one for each index of `group`. A program takes and returns all parts, laid end to end along the dimension named above; an argument that names none is the same for every part. Nothing has to cross between parts.
Inputs may be any that keep to these rules, and one draw needn't show every extreme that they name: `far_rows`: slots of device block d name leaves d * 16 to (d + 1) * 16 - 1; each block's live slots come first, then -1; one block in every draw fills all 256 slots. `far_cols`: -1 exactly where far_rows is -1; a live column leaf never lies on the device block of its row leaf; the live column leaves of one device block that lie on any one device block are at most 4 distinct leaves, and some pair of blocks reaches 4 in every draw.
All inputs are finite; a program needn't handle non-finite values.
Results may differ from a plain program's by a relative error of at most 0.0054.
Values may be sent and summed in bfloat16 or wider, within the bound.
A program may use at most 64 MiB of HBM per device.

v0:
```python
import functools

import jax
import jax.numpy as jnp
from jax import lax
from jax.experimental import pallas as pl
from jax.experimental.pallas import tpu as pltpu
from jax.sharding import PartitionSpec as P

NEED = 4
LANES = 128
F32 = jnp.float32
BF16 = jnp.bfloat16
LAST = (((1,), (1,)), ((), ()))
FIRST = (((0,), (0,)), ((), ()))


def dot(x, y):
    return jnp.dot(x, y, preferred_element_type=F32)


def dot_last(x, y):
    return lax.dot_general(x, y, LAST, preferred_element_type=F32)


def iota(shape, dim):
    return lax.broadcasted_iota(jnp.int32, shape, dim)


def flag(condition):
    return jnp.where(condition, 1.0, 0.0).astype(BF16)


def kernel(
    n, inner, members, leaves, rank, leaf, tasks,
    anomalies, order, bases_hbm, near_hbm, far_rows, far_cols, coupling_hbm,
    out,
    bases, near, coupling, cols_all, halo, tree, one_hot, selector, chosen, table,
    turned, picked, near_field, placing, combined,
    load_sems, near_sems, cols_send, cols_recv, halo_send, halo_recv, coef_send, coef_recv,
):
    me = lax.axis_index("row") * inner + lax.axis_index("col")
    width = leaves * leaf
    split = leaf // rank
    groups = members // split
    rows = NEED * groups
    per = leaf // rows
    blocks = n // per
    halves = tasks // LANES

    def at(index):
        return {"row": index // inner, "col": lax.rem(index, inner)}

    def peer(step):
        return lax.rem(me + step, n)

    barrier = pltpu.get_barrier_semaphore()

    def greet(step, carry):
        pl.semaphore_signal(barrier, inc=1, device_id=at(peer(step)), device_id_type=pl.DeviceIdType.MESH)
        return carry

    lax.fori_loop(1, n, greet, 0)

    load_bases = pltpu.make_async_copy(bases_hbm, bases, load_sems.at[0])
    load_bases.start()
    quarter = leaves // 4
    loads = []
    for q in range(4):
        part = pl.ds(q * quarter, quarter)
        loads.append(pltpu.make_async_copy(near_hbm.at[part], near.at[part], near_sems.at[q]))
        loads[-1].start()
    load_coupling = pltpu.make_async_copy(coupling_hbm.at[0], coupling, load_sems.at[1])
    load_coupling.start()

    position = order[...]
    low = position % leaf
    high = position // leaf
    for c in range(leaves):
        piece = slice(c * leaf, (c + 1) * leaf)
        one_hot[:, piece] = flag(iota((leaf, leaf), 0) == low[:, piece])

    pl.semaphore_wait(barrier, n - 1)

    def cols_copy(step):
        return pltpu.make_async_remote_copy(
            src_ref=far_cols, dst_ref=cols_all.at[me],
            send_sem=cols_send.at[step], recv_sem=cols_recv.at[step],
            device_id=at(peer(step)), device_id_type=pl.DeviceIdType.MESH,
        )

    def cols_start(step, carry):
        cols_copy(step).start()
        return carry

    lax.fori_loop(1, n, cols_start, 0)
    cols_all[me] = jnp.full((1, tasks), -1, jnp.int32)

    stacked = jnp.concatenate(
        [anomalies[:, s * leaf : (s + 1) * leaf] for s in range(leaves)], axis=0
    )
    for c in range(leaves):
        piece = slice(c * leaf, (c + 1) * leaf)
        spread = dot(stacked, one_hot[:, piece])
        where_high = high[:, piece]
        total = jnp.zeros((members, leaf), F32)
        for s in range(leaves):
            total = total + jnp.where(where_high == s, spread[s * members : (s + 1) * members], 0.0)
        tree[:, piece] = total.astype(BF16)

    to_next = pltpu.make_async_remote_copy(
        src_ref=tree.at[:, pl.ds((leaves - 1) * leaf, leaf)], dst_ref=halo.at[0],
        send_sem=halo_send.at[0], recv_sem=halo_recv.at[0],
        device_id=at(peer(1)), device_id_type=pl.DeviceIdType.MESH,
    )
    to_before = pltpu.make_async_remote_copy(
        src_ref=tree.at[:, pl.ds(0, leaf)], dst_ref=halo.at[1],
        send_sem=halo_send.at[1], recv_sem=halo_recv.at[1],
        device_id=at(peer(n - 1)), device_id_type=pl.DeviceIdType.MESH,
    )
    to_next.start()
    to_before.start()

    load_bases.wait()
    upward = jnp.concatenate(
        [dot_last(tree[:, t * leaf : (t + 1) * leaf], bases[t]) for t in range(leaves)], axis=0
    ).astype(BF16)
    repeat = flag(iota((rank, leaf), 0) == iota((rank, leaf), 1) % rank)
    square = (leaf, leaf)
    row, col = iota(square, 0), iota(square, 1)
    spread = dot(upward, repeat)
    placed = jnp.where(row % split == col // rank, spread, 0.0).astype(BF16)

    same = row // rows == col // rows
    gather = flag(same)
    earlier = flag(same & (col < row))
    ones = jnp.ones((tasks, leaf), BF16)
    slot = (row % rows) // groups + 1
    group_row = row % groups

    def ranks(hits):
        needed = jnp.minimum(dot(hits, ones), 1.0)
        return needed, dot(earlier, needed.astype(BF16)) + 1.0

    def cols_wait(step, carry):
        cols_copy(step).wait()
        return carry

    lax.fori_loop(1, n, cols_wait, 0)
    slot_f = slot.astype(F32)
    diagonal = row % leaves == col // members
    same_group = group_row == (col % members) // split
    for c in range(blocks):
        wanted = jnp.concatenate(
            [jnp.broadcast_to(cols_all[c * per + d], (leaves, tasks)) for d in range(per)], axis=0
        )
        hits = flag(wanted == iota((leaf, tasks), 0) % leaves + me * leaves)
        needed, numbered = ranks(hits)
        values = jnp.where(diagonal, needed * numbered, 0.0).astype(BF16)
        rank_of = dot(gather, values)
        selection = flag((rank_of == slot_f) & same_group)
        chosen[c * leaf : (c + 1) * leaf, :] = dot(selection, placed).astype(BF16)

    def coef_copy(step):
        there = peer(step)
        return pltpu.make_async_remote_copy(
            src_ref=chosen.at[pl.ds(pl.multiple_of(there * rows, rows), rows)],
            dst_ref=table.at[pl.ds(pl.multiple_of(me * rows, rows), rows)],
            send_sem=coef_send.at[step], recv_sem=coef_recv.at[step],
            device_id=at(there), device_id_type=pl.DeviceIdType.MESH,
        )

    def coef_start(step, carry):
        coef_copy(step).start()
        return carry

    lax.fori_loop(1, n, coef_start, 0)
    table[pl.ds(pl.multiple_of(me * rows, rows), rows), :] = jnp.zeros((rows, leaf), BF16)

    own = far_cols[...]
    for c in range(blocks):
        hits = own == iota((leaf, tasks), 0) + c * leaf
        needed, numbered = ranks(flag(hits))
        rank_of = dot(gather, jnp.where(hits, numbered, 0.0).astype(BF16))
        selector[c * leaf : (c + 1) * leaf, :] = jnp.where(rank_of == slot_f, 1.0, 0.0).astype(BF16)
    placing[...] = flag(far_rows[...] == iota((leaf, tasks), 0) // members + me * leaves)

    to_next.wait()
    to_before.wait()
    before = jnp.where(me > 0, halo[0].astype(F32), 0.0).astype(BF16)
    after = jnp.where(me < n - 1, halo[1].astype(F32), 0.0).astype(BF16)
    for t in range(leaves):
        if t % quarter == 0:
            loads[t // quarter].wait()
        total = jnp.zeros((members, leaf), F32)
        for j in range(3):
            s = t + j - 1
            if s < 0:
                x = before
            elif s >= leaves:
                x = after
            else:
                x = tree[:, s * leaf : (s + 1) * leaf]
            total = total + dot_last(x, near[t, j])
        near_field[:, t * leaf : (t + 1) * leaf] = total

    load_coupling.wait()
    identity = flag(row == col)
    for c in range(rank * rank // leaf):
        piece = slice(c * leaf, (c + 1) * leaf)
        flipped = dot_last(identity, coupling[:, piece])
        for h in range(halves):
            turned[h, piece, :] = flipped[:, h * LANES : (h + 1) * LANES]

    def coef_wait(step, carry):
        coef_copy(step).wait()
        return carry

    lax.fori_loop(1, n, coef_wait, 0)
    for g in range(groups):
        total = jnp.zeros((leaf, tasks), F32)
        for c in range(blocks):
            chunk = slice(c * leaf, (c + 1) * leaf)
            taken = jnp.where(group_row == g, selector[chunk, :].astype(F32), 0.0).astype(BF16)
            total = total + lax.dot_general(table[chunk, :], taken, FIRST, preferred_element_type=F32)
        for h in range(halves):
            picked[h, g * leaf : (g + 1) * leaf, :] = total[:, h * LANES : (h + 1) * LANES]

    together = 4

    def advance(step, total):
        left = []
        right = []
        for u in range(together):
            b = step * together + u
            for h in range(halves):
                values = picked[h, pl.ds(b, members, stride=rank), :].astype(BF16)
                mask = placing[:, h * LANES : (h + 1) * LANES]
                left.append(jnp.concatenate([values] * leaves, axis=0) * mask)
                right.append(turned[h, pl.ds(b, rank, stride=rank), :].astype(BF16))
        return total + dot_last(jnp.concatenate(left, axis=1), jnp.concatenate(right, axis=1))

    far = lax.fori_loop(0, rank // together, advance, jnp.zeros((leaves * members, rank), F32))
    far = far.astype(BF16)
    for t in range(leaves):
        piece = slice(t * leaf, (t + 1) * leaf)
        value = near_field[:, piece] + dot(far[t * members : (t + 1) * members], bases[t])
        combined[:, piece] = value.astype(BF16)

    total = jnp.zeros((leaves * members, leaf), F32)
    for c in range(leaves):
        piece = slice(c * leaf, (c + 1) * leaf)
        values = combined[:, piece].astype(F32)
        where_high = high[:, piece]
        left = jnp.concatenate(
            [jnp.where(where_high == s, values, 0.0).astype(BF16) for s in range(leaves)], axis=0
        )
        total = total + dot_last(left, one_hot[:, piece])
    for s in range(leaves):
        out[:, s * leaf : (s + 1) * leaf] = total[s * members : (s + 1) * members].astype(BF16)


def body(n, inner, anomalies, order, bases, near_blocks, far_rows, far_cols, coupling):
    members, points = anomalies.shape
    leaves, rank, leaf = bases.shape
    tasks = far_cols.shape[1]
    rows = NEED * members * rank // leaf
    vmem = pl.BlockSpec(memory_space=pltpu.VMEM)
    hbm = pl.BlockSpec(memory_space=pl.ANY)
    dma = pltpu.SemaphoreType.DMA
    return pl.pallas_call(
        functools.partial(kernel, n, inner, members, leaves, rank, leaf, tasks),
        out_shape=jax.ShapeDtypeStruct((members, points), BF16),
        in_specs=[vmem, vmem, hbm, hbm, vmem, vmem, hbm],
        out_specs=vmem,
        scratch_shapes=[
            pltpu.VMEM(bases.shape, BF16),
            pltpu.VMEM(near_blocks.shape, BF16),
            pltpu.VMEM((tasks, rank * rank), BF16),
            pltpu.VMEM((n, 1, tasks), jnp.int32),
            pltpu.VMEM((2, members, leaf), BF16),
            pltpu.VMEM((members, points), BF16),
            pltpu.VMEM((leaf, points), BF16),
            pltpu.VMEM((n * rows, tasks), BF16),
            pltpu.VMEM((n * rows, leaf), BF16),
            pltpu.VMEM((n * rows, leaf), BF16),
            pltpu.VMEM((tasks // LANES, rank * rank, LANES), F32),
            pltpu.VMEM((tasks // LANES, members * rank, LANES), F32),
            pltpu.VMEM((members, points), F32),
            pltpu.VMEM((leaves * members, tasks), BF16),
            pltpu.VMEM((members, points), BF16),
            dma((2,)), dma((4,)), dma((n,)), dma((n,)), dma((2,)), dma((2,)), dma((n,)), dma((n,)),
        ],
        compiler_params=pltpu.CompilerParams(
            collective_id=0, has_side_effects=True, vmem_limit_bytes=40 * 1024 * 1024
        ),
    )(anomalies, order, bases, near_blocks, far_rows, far_cols, coupling)


def solution(mesh):
    rows, inner = mesh.shape["row"], mesh.shape["col"]
    spread = ("row", "col")
    in_specs = (
        P("group", spread),
        P(spread, None),
        P(spread, None, None),
        P(spread, None, None, None),
        P(spread, None),
        P(spread, None),
        P(spread, None, None),
    )
    return jax.shard_map(
        functools.partial(body, rows * inner, inner),
        mesh=mesh, in_specs=in_specs, out_specs=P("group", spread), check_vma=False,
    )
```

profile of v0, /device:TPU:0, one launch (start us, length us, event | category | flops | bytes accessed | tf_op | source)
XLA Modules:
  0.0 32.8 jit_solution(4928027508928495689)
XLA Ops:
  0.0 0.0 copy-start
  0.0 2.8 %copy-done = bf16[16,3,256,256]{3,2,1,0:T(8,128)(2,1)S(1)} copy-done((bf16[16,3,256,256]{3,2,1,0:T(8,128)(2,1)S(1)}, bf16[16,3,256,256]{3,2,1,0:T(8,128)(2,1)}, u32[]{:S(2)}) %copy-start) | copy-done | bytes 6291480
  2.8 0.0 copy-start.1
  2.8 1.6 %copy-done.1 = bf16[1,256,4096]{2,1,0:T(8,128)(2,1)S(1)} copy-done((bf16[1,256,4096]{2,1,0:T(8,128)(2,1)S(1)}, bf16[1,256,4096]{2,1,0:T(8,128)(2,1)}, u32[]{:S(2)}) %copy-start.1) | copy-done | bytes 2097176
  4.4 0.0 copy-start.2
  4.4 1.0 %copy-done.2 = bf16[16,64,256]{2,1,0:T(8,128)(2,1)S(1)} copy-done((bf16[16,64,256]{2,1,0:T(8,128)(2,1)S(1)}, bf16[16,64,256]{2,1,0:T(8,128)(2,1)}, u32[]{:S(2)}) %copy-start.2) | copy-done | bytes 524312
  5.4 0.0 copy-start.3
  5.4 0.9 %copy-done.3 = bf16[16,4096]{1,0:T(8,128)(2,1)S(1)} copy-done((bf16[16,4096]{1,0:T(8,128)(2,1)S(1)}, bf16[16,4096]{1,0:T(8,128)(2,1)}, u32[]{:S(2)}) %copy-start.3) | copy-done | bytes 131096
  6.3 0.0 copy-start.4
  6.3 0.7 %copy-done.4 = s32[1,4096]{1,0:T(1,128)S(1)} copy-done((s32[1,4096]{1,0:T(1,128)S(1)}, s32[1,4096]{1,0:T(1,128)}, u32[]{:S(2)}) %copy-start.4) | copy-done | bytes 16408
  7.0 0.0 copy-start.5
  7.0 0.7 %copy-done.5 = s32[1,256]{1,0:T(1,128)S(1)} copy-done((s32[1,256]{1,0:T(1,128)S(1)}, s32[1,256]{1,0:T(1,128)}, u32[]{:S(2)}) %copy-start.5) | copy-done | bytes 1048
  7.7 0.0 copy-start.6
  7.7 0.7 %copy-done.6 = s32[1,256]{1,0:T(1,128)S(1)} copy-done((s32[1,256]{1,0:T(1,128)S(1)}, s32[1,256]{1,0:T(1,128)}, u32[]{:S(2)}) %copy-start.6) | copy-done | bytes 1048
  8.4 23.8 %shard_map.73 = bf16[16,4096]{1,0:T(8,128)(2,1)S(1)} custom-call(bf16[16,4096]{1,0:T(8,128)(2,1)S(1)} %copy-done.3, s32[1,4096]{1,0:T(1,128)S(1)} %copy-done.4, bf16[16,64,256]{2,1,0:T(8,128)(2,1)S(1)} %copy-done.2, bf16[16,3,256,256]{3,2,1,0:T(8,128)(2,1)S(1)} %copy-done, s32[1,256]{1,0:T(1,128)S(1)} %copy-done.5, s32[1,256]{1,0:T(1,128)S(1)} %copy-done.6, ...), custom_call_target="tpu_custom_call" | custom-call | tf_op jit(solution)/shard_map/pallas_call | solution.py:271
  32.2 0.7 %copy.9 = bf16[16,4096]{1,0:T(8,128)(2,1)} copy(bf16[16,4096]{1,0:T(8,128)(2,1)S(1)} %shard_map.73) | data formatting | bytes 262144
Async XLA Ops:
  0.0 2.8 %copy-start = (bf16[16,3,256,256]{3,2,1,0:T(8,128)(2,1)S(1)}, bf16[16,3,256,256]{3,2,1,0:T(8,128)(2,1)}, u32[]{:S(2)}) copy-start(bf16[16,3,256,256]{3,2,1,0:T(8,128)(2,1)} %near_hbm.1) | copy-start | bytes 18874372
  2.8 1.6 %copy-start.1 = (bf16[1,256,4096]{2,1,0:T(8,128)(2,1)S(1)}, bf16[1,256,4096]{2,1,0:T(8,128)(2,1)}, u32[]{:S(2)}) copy-start(bf16[1,256,4096]{2,1,0:T(8,128)(2,1)} %coupling_hbm.1) | copy-start | bytes 6291460
  4.4 1.0 %copy-start.2 = (bf16[16,64,256]{2,1,0:T(8,128)(2,1)S(1)}, bf16[16,64,256]{2,1,0:T(8,128)(2,1)}, u32[]{:S(2)}) copy-start(bf16[16,64,256]{2,1,0:T(8,128)(2,1)} %bases_hbm.1) | copy-start | bytes 1572868
  5.4 0.9 %copy-start.3 = (bf16[16,4096]{1,0:T(8,128)(2,1)S(1)}, bf16[16,4096]{1,0:T(8,128)(2,1)}, u32[]{:S(2)}) copy-start(bf16[16,4096]{1,0:T(8,128)(2,1)} %anomalies.1) | copy-start | bytes 393220
  6.3 0.7 %copy-start.4 = (s32[1,4096]{1,0:T(1,128)S(1)}, s32[1,4096]{1,0:T(1,128)}, u32[]{:S(2)}) copy-start(s32[1,4096]{1,0:T(1,128)} %order.1) | copy-start | bytes 49156
  7.0 0.7 %copy-start.5 = (s32[1,256]{1,0:T(1,128)S(1)}, s32[1,256]{1,0:T(1,128)}, u32[]{:S(2)}) copy-start(s32[1,256]{1,0:T(1,128)} %far_rows.1) | copy-start | bytes 3076
  7.7 0.7 %copy-start.6 = (s32[1,256]{1,0:T(1,128)S(1)}, s32[1,256]{1,0:T(1,128)}, u32[]{:S(2)}) copy-start(s32[1,256]{1,0:T(1,128)} %far_cols.1) | copy-start | bytes 3076
where the time goes:
time: 33.2 us; the launch traced here: 32.8 us
  Pallas kernels  23.8 us (72%)
  local copies, waits for them, and re-layouts  9.05 us (27%)
    pallas_call x1, Pallas kernels, body(): pl.pallas_call(functools.partial(kernel, n, inner, members, leaves, rank,...  23.8 us
    unnamed x15, local copies, waits for them, and re-layouts  9.05 us

commit v1 on v0

--- a/solution.py
+++ b/solution.py
@@ -33,11 +33,11 @@
 
 def kernel(
     n, inner, members, leaves, rank, leaf, tasks,
-    anomalies, order, bases_hbm, near_hbm, far_rows, far_cols, coupling_hbm,
+    anomalies_hbm, order_hbm, bases_hbm, near_hbm, far_rows_hbm, far_cols_hbm, coupling_hbm,
     out,
-    bases, near, coupling, cols_all, halo, tree, one_hot, selector, chosen, table,
+    anomalies, order, far_rows, far_cols, bases, near, coupling, cols_all, halo, tree, one_hot, selector, chosen, table,
     turned, picked, near_field, placing, combined,
-    load_sems, near_sems, cols_send, cols_recv, halo_send, halo_recv, coef_send, coef_recv,
+    small_sems, load_sems, near_sems, cols_send, cols_recv, halo_send, halo_recv, coef_send, coef_recv,
 ):
     me = lax.axis_index("row") * inner + lax.axis_index("col")
     width = leaves * leaf
@@ -62,6 +62,11 @@
 
     lax.fori_loop(1, n, greet, 0)
 
+    small = []
+    pairs = ((order_hbm, order), (anomalies_hbm, anomalies), (far_cols_hbm, far_cols), (far_rows_hbm, far_rows))
+    for i, (source, target) in enumerate(pairs):
+        small.append(pltpu.make_async_copy(source, target, small_sems.at[i]))
+        small[-1].start()
     load_bases = pltpu.make_async_copy(bases_hbm, bases, load_sems.at[0])
     load_bases.start()
     quarter = leaves // 4
@@ -73,6 +78,7 @@
     load_coupling = pltpu.make_async_copy(coupling_hbm.at[0], coupling, load_sems.at[1])
     load_coupling.start()
 
+    small[0].wait()
     position = order[...]
     low = position % leaf
     high = position // leaf
@@ -84,7 +90,7 @@
 
     def cols_copy(step):
         return pltpu.make_async_remote_copy(
-            src_ref=far_cols, dst_ref=cols_all.at[me],
+            src_ref=far_cols_hbm, dst_ref=cols_all.at[me],
             send_sem=cols_send.at[step], recv_sem=cols_recv.at[step],
             device_id=at(peer(step)), device_id_type=pl.DeviceIdType.MESH,
         )
@@ -96,6 +102,7 @@
     lax.fori_loop(1, n, cols_start, 0)
     cols_all[me] = jnp.full((1, tasks), -1, jnp.int32)
 
+    small[1].wait()
     stacked = jnp.concatenate(
         [anomalies[:, s * leaf : (s + 1) * leaf] for s in range(leaves)], axis=0
     )
@@ -177,6 +184,8 @@
     lax.fori_loop(1, n, coef_start, 0)
     table[pl.ds(pl.multiple_of(me * rows, rows), rows), :] = jnp.zeros((rows, leaf), BF16)
 
+    small[2].wait()
+    small[3].wait()
     own = far_cols[...]
     for c in range(blocks):
         hits = own == iota((leaf, tasks), 0) + c * leaf
@@ -266,14 +275,18 @@
     tasks = far_cols.shape[1]
     rows = NEED * members * rank // leaf
     vmem = pl.BlockSpec(memory_space=pltpu.VMEM)
-    hbm = pl.BlockSpec(memory_space=pl.ANY)
+    hbm = pl.BlockSpec(memory_space=pltpu.HBM)
     dma = pltpu.SemaphoreType.DMA
     return pl.pallas_call(
         functools.partial(kernel, n, inner, members, leaves, rank, leaf, tasks),
         out_shape=jax.ShapeDtypeStruct((members, points), BF16),
-        in_specs=[vmem, vmem, hbm, hbm, vmem, vmem, hbm],
+        in_specs=[hbm] * 7,
         out_specs=vmem,
         scratch_shapes=[
+            pltpu.VMEM(anomalies.shape, BF16),
+            pltpu.VMEM(order.shape, jnp.int32),
+            pltpu.VMEM(far_rows.shape, jnp.int32),
+            pltpu.VMEM(far_cols.shape, jnp.int32),
             pltpu.VMEM(bases.shape, BF16),
             pltpu.VMEM(near_blocks.shape, BF16),
             pltpu.VMEM((tasks, rank * rank), BF16),
@@ -289,10 +302,10 @@
             pltpu.VMEM((members, points), F32),
             pltpu.VMEM((leaves * members, tasks), BF16),
             pltpu.VMEM((members, points), BF16),
-            dma((2,)), dma((4,)), dma((n,)), dma((n,)), dma((2,)), dma((2,)), dma((n,)), dma((n,)),
+            dma((4,)), dma((2,)), dma((4,)), dma((n,)), dma((n,)), dma((2,)), dma((2,)), dma((n,)), dma((n,)),
         ],
         compiler_params=pltpu.CompilerParams(
-            collective_id=0, has_side_effects=True, vmem_limit_bytes=40 * 1024 * 1024
+            collective_id=0, has_side_effects=True, vmem_limit_bytes=60 * 1024 * 1024
         ),
     )(anomalies, order, bases, near_blocks, far_rows, far_cols, coupling)
 

time: 33.2 us -> 26.9 us (0.81)
  local copies, waits for them, and re-layouts: 9.05 us -> 1.57 us
  Pallas kernels: 23.8 us -> 25.1 us
    unnamed x15 -> x1, local copies, waits for them, and re-layouts: 9.05 us -> 1.57 us
    pallas_call x1, Pallas kernels: 23.8 us -> 25.1 us  [body(): pl.pallas_call(functools.partial(kernel, n, inner, members, leaves, rank,...]
where the time goes in v1:
time: 26.9 us; the launch traced here: 26.7 us
  Pallas kernels  25.1 us (93%)
  local copies, waits for them, and re-layouts  1.57 us (6%)
    pallas_call x1, Pallas kernels, body(): pl.pallas_call(functools.partial(kernel, n, inner, members, leaves, rank,...  25.1 us
    unnamed x1, local copies, waits for them, and re-layouts  1.57 us

profile of v1, /device:TPU:0, one launch (start us, length us, event | category | flops | bytes accessed | tf_op | source)
XLA Modules:
  0.0 26.7 jit_solution(1111981871624436096)
XLA Ops:
  0.0 25.1 %shard_map.73 = bf16[16,4096]{1,0:T(8,128)(2,1)} custom-call(bf16[16,4096]{1,0:T(8,128)(2,1)} %anomalies_hbm.1, s32[1,4096]{1,0:T(1,128)} %order_hbm.1, bf16[16,64,256]{2,1,0:T(8,128)(2,1)} %bases_hbm.1, bf16[16,3,256,256]{3,2,1,0:T(8,128)(2,1)} %near_hbm.1, s32[1,256]{1,0:T(1,128)} %far_rows_hbm.1, s32[1,256]{1,0:T(1,128)} %far_cols_hbm.1, ...), custom_call_target="tpu_custom_call" | custom-call | tf_op jit(solution)/shard_map/pallas_call | solution.py:280
  25.1 1.6 %copy.9 = bf16[16,4096]{1,0:T(8,128)(2,1)} copy(bf16[16,4096]{1,0:T(8,128)(2,1)} %shard_map.73) | data formatting | bytes 262144

commit v2 on v1

--- a/solution.py
+++ b/solution.py
@@ -235,7 +235,7 @@
         for h in range(halves):
             picked[h, g * leaf : (g + 1) * leaf, :] = total[:, h * LANES : (h + 1) * LANES]
 
-    together = 4
+    together = 32
 
     def advance(step, total):
         left = []
@@ -247,10 +247,10 @@
                 mask = placing[:, h * LANES : (h + 1) * LANES]
                 left.append(jnp.concatenate([values] * leaves, axis=0) * mask)
                 right.append(turned[h, pl.ds(b, rank, stride=rank), :].astype(BF16))
-        return total + dot_last(jnp.concatenate(left, axis=1), jnp.concatenate(right, axis=1))
-
-    far = lax.fori_loop(0, rank // together, advance, jnp.zeros((leaves * members, rank), F32))
-    far = far.astype(BF16)
+        return total + dot_last(jnp.concatenate(right, axis=1), jnp.concatenate(left, axis=1))
+
+    far = lax.fori_loop(0, rank // together, advance, jnp.zeros((rank, leaves * members), F32))
+    far = far.T.astype(BF16)
     for t in range(leaves):
         piece = slice(t * leaf, (t + 1) * leaf)
         value = near_field[:, piece] + dot(far[t * members : (t + 1) * members], bases[t])

time: 26.9 us -> 23.2 us (0.86)
  Pallas kernels: 25.1 us -> 21.4 us
    pallas_call x1, Pallas kernels: 25.1 us -> 21.4 us  [body(): pl.pallas_call(functools.partial(kernel, n, inner, members, leaves, rank,...]
where the time goes in v2:
time: 23.2 us; the launch traced here: 22.9 us
  Pallas kernels  21.4 us (92%)
  local copies, waits for them, and re-layouts  1.57 us (7%)
    pallas_call x1, Pallas kernels, body(): pl.pallas_call(functools.partial(kernel, n, inner, members, leaves, rank,...  21.4 us
    unnamed x1, local copies, waits for them, and re-layouts  1.57 us

profile of v2, /device:TPU:0, one launch (start us, length us, event | category | flops | bytes accessed | tf_op | source)
XLA Modules:
  0.0 22.9 jit_solution(448000633849583081)
XLA Ops:
  0.0 21.4 %shard_map.73 = bf16[16,4096]{1,0:T(8,128)(2,1)} custom-call(bf16[16,4096]{1,0:T(8,128)(2,1)} %anomalies_hbm.1, s32[1,4096]{1,0:T(1,128)} %order_hbm.1, bf16[16,64,256]{2,1,0:T(8,128)(2,1)} %bases_hbm.1, bf16[16,3,256,256]{3,2,1,0:T(8,128)(2,1)} %near_hbm.1, s32[1,256]{1,0:T(1,128)} %far_rows_hbm.1, s32[1,256]{1,0:T(1,128)} %far_cols_hbm.1, ...), custom_call_target="tpu_custom_call" | custom-call | tf_op jit(solution)/shard_map/pallas_call | solution.py:280
  21.4 1.6 %copy.9 = bf16[16,4096]{1,0:T(8,128)(2,1)} copy(bf16[16,4096]{1,0:T(8,128)(2,1)} %shard_map.73) | data formatting | bytes 262144

commit v3 on v2

--- a/solution.py
+++ b/solution.py
@@ -36,7 +36,7 @@
     anomalies_hbm, order_hbm, bases_hbm, near_hbm, far_rows_hbm, far_cols_hbm, coupling_hbm,
     out,
     anomalies, order, far_rows, far_cols, bases, near, coupling, cols_all, halo, tree, one_hot, selector, chosen, table,
-    turned, picked, near_field, placing, combined,
+    placed, turned, picked, near_field, placing, combined,
     small_sems, load_sems, near_sems, cols_send, cols_recv, halo_send, halo_recv, coef_send, coef_recv,
 ):
     me = lax.axis_index("row") * inner + lax.axis_index("col")
@@ -78,13 +78,43 @@
     load_coupling = pltpu.make_async_copy(coupling_hbm.at[0], coupling, load_sems.at[1])
     load_coupling.start()
 
-    small[0].wait()
-    position = order[...]
-    low = position % leaf
-    high = position // leaf
-    for c in range(leaves):
-        piece = slice(c * leaf, (c + 1) * leaf)
-        one_hot[:, piece] = flag(iota((leaf, leaf), 0) == low[:, piece])
+    square = (leaf, leaf)
+    row, col = iota(square, 0), iota(square, 1)
+    early = me < n // 2
+
+    def upward_pass():
+        small[0].wait()
+        position = order[...]
+        low = position % leaf
+        high = position // leaf
+        for c in range(leaves):
+            piece = slice(c * leaf, (c + 1) * leaf)
+            one_hot[:, piece] = flag(iota((leaf, leaf), 0) == low[:, piece])
+
+        small[1].wait()
+        stacked = jnp.concatenate(
+            [anomalies[:, s * leaf : (s + 1) * leaf] for s in range(leaves)], axis=0
+        )
+        for c in range(leaves):
+            piece = slice(c * leaf, (c + 1) * leaf)
+            spread = dot(stacked, one_hot[:, piece])
+            where_high = high[:, piece]
+            total = jnp.zeros((members, leaf), F32)
+            for s in range(leaves):
+                total = total + jnp.where(where_high == s, spread[s * members : (s + 1) * members], 0.0)
+            tree[:, piece] = total.astype(BF16)
+
+        load_bases.wait()
+        upward = jnp.concatenate(
+            [dot_last(tree[:, t * leaf : (t + 1) * leaf], bases[t]) for t in range(leaves)], axis=0
+        ).astype(BF16)
+        repeat = flag(iota((rank, leaf), 0) == iota((rank, leaf), 1) % rank)
+        spread = dot(upward, repeat)
+        placed[...] = jnp.where(row % split == col // rank, spread, 0.0).astype(BF16)
+
+    @pl.when(early)
+    def _():
+        upward_pass()
 
     pl.semaphore_wait(barrier, n - 1)
 
@@ -102,18 +132,9 @@
     lax.fori_loop(1, n, cols_start, 0)
     cols_all[me] = jnp.full((1, tasks), -1, jnp.int32)
 
-    small[1].wait()
-    stacked = jnp.concatenate(
-        [anomalies[:, s * leaf : (s + 1) * leaf] for s in range(leaves)], axis=0
-    )
-    for c in range(leaves):
-        piece = slice(c * leaf, (c + 1) * leaf)
-        spread = dot(stacked, one_hot[:, piece])
-        where_high = high[:, piece]
-        total = jnp.zeros((members, leaf), F32)
-        for s in range(leaves):
-            total = total + jnp.where(where_high == s, spread[s * members : (s + 1) * members], 0.0)
-        tree[:, piece] = total.astype(BF16)
+    @pl.when(jnp.logical_not(early))
+    def _():
+        upward_pass()
 
     to_next = pltpu.make_async_remote_copy(
         src_ref=tree.at[:, pl.ds((leaves - 1) * leaf, leaf)], dst_ref=halo.at[0],
@@ -128,16 +149,6 @@
     to_next.start()
     to_before.start()
 
-    load_bases.wait()
-    upward = jnp.concatenate(
-        [dot_last(tree[:, t * leaf : (t + 1) * leaf], bases[t]) for t in range(leaves)], axis=0
-    ).astype(BF16)
-    repeat = flag(iota((rank, leaf), 0) == iota((rank, leaf), 1) % rank)
-    square = (leaf, leaf)
-    row, col = iota(square, 0), iota(square, 1)
-    spread = dot(upward, repeat)
-    placed = jnp.where(row % split == col // rank, spread, 0.0).astype(BF16)
-
     same = row // rows == col // rows
     gather = flag(same)
     earlier = flag(same & (col < row))
@@ -166,7 +177,7 @@
         values = jnp.where(diagonal, needed * numbered, 0.0).astype(BF16)
         rank_of = dot(gather, values)
         selection = flag((rank_of == slot_f) & same_group)
-        chosen[c * leaf : (c + 1) * leaf, :] = dot(selection, placed).astype(BF16)
+        chosen[c * leaf : (c + 1) * leaf, :] = dot(selection, placed[...]).astype(BF16)
 
     def coef_copy(step):
         there = peer(step)
@@ -260,7 +271,7 @@
     for c in range(leaves):
         piece = slice(c * leaf, (c + 1) * leaf)
         values = combined[:, piece].astype(F32)
-        where_high = high[:, piece]
+        where_high = order[:, piece] // leaf
         left = jnp.concatenate(
             [jnp.where(where_high == s, values, 0.0).astype(BF16) for s in range(leaves)], axis=0
         )
@@ -297,6 +308,7 @@
             pltpu.VMEM((n * rows, tasks), BF16),
             pltpu.VMEM((n * rows, leaf), BF16),
             pltpu.VMEM((n * rows, leaf), BF16),
+            pltpu.VMEM((leaf, leaf), BF16),
             pltpu.VMEM((tasks // LANES, rank * rank, LANES), F32),
             pltpu.VMEM((tasks // LANES, members * rank, LANES), F32),
             pltpu.VMEM((members, points), F32),

time: 23.2 us -> 23.2 us (level)
  no operation moved by 1% of the time
where the time goes in v3:
time: 23.2 us; the launch traced here: 23 us
  Pallas kernels  21.4 us (92%)
  local copies, waits for them, and re-layouts  1.57 us (7%)
    pallas_call x1, Pallas kernels, body(): pl.pallas_call(functools.partial(kernel, n, inner, members, leaves, rank,...  21.4 us
    unnamed x1, local copies, waits for them, and re-layouts  1.57 us

profile of v3, /device:TPU:0, one launch (start us, length us, event | category | flops | bytes accessed | tf_op | source)
XLA Modules:
  0.0 23.0 jit_solution(9554849332093010406)
XLA Ops:
  0.0 21.4 %shard_map.73 = bf16[16,4096]{1,0:T(8,128)(2,1)} custom-call(bf16[16,4096]{1,0:T(8,128)(2,1)} %anomalies_hbm.1, s32[1,4096]{1,0:T(1,128)} %order_hbm.1, bf16[16,64,256]{2,1,0:T(8,128)(2,1)} %bases_hbm.1, bf16[16,3,256,256]{3,2,1,0:T(8,128)(2,1)} %near_hbm.1, s32[1,256]{1,0:T(1,128)} %far_rows_hbm.1, s32[1,256]{1,0:T(1,128)} %far_cols_hbm.1, ...), custom_call_target="tpu_custom_call" | custom-call | tf_op jit(solution)/shard_map/pallas_call | solution.py:291
  21.4 1.6 %copy.9 = bf16[16,4096]{1,0:T(8,128)(2,1)} copy(bf16[16,4096]{1,0:T(8,128)(2,1)} %shard_map.73) | data formatting | bytes 262144
